TPU v7x, 32 devices: a whole 2x2x4 slice. The times are simulated.
32 devices in a mesh: sx: 4 (over y, x), sy: 8 (over z, core).
Axes of the slice: x: 2, y: 2, z: 4, core: 2. Of those that a mesh axis runs over, the one named last changes fastest.
Arguments:
- interior_rhs: bfloat16 [4, 8, 2048, 1024], P('sx', 'sy'), may hold values from -6 to 6
- interface_coupling: bfloat16 [4, 8, 1024, 2048], P('sx', 'sy'), may hold values from -0.125 to 0.125
- interface_local: float32 [4, 8, 1024, 1024], P('sx', 'sy'), may hold values from -6 to 6
- off_blocks: bfloat16 [4, 8, 16, 4, 128, 128], P('sx', 'sy'), may hold values from -0.125 to 0.125
- diag_inverse: bfloat16 [4, 8, 16, 128, 128], P('sx', 'sy')
- block_pattern: int32 [4, 8, 16, 4], P('sx', 'sy'), may hold values from 0 to 15
- face_order: int32 [4, 8, 2, 512], P('sx', 'sy'), may hold values from 0 to 511, each once within a row
- krylov_map: int32 [4, 8, 1024], P('sx', 'sy'), may hold values from 0 to 1023, each once within a row
Outputs:
- krylov_rows: float32 [4, 8, 1024, 1024], P('sx', 'sy')
Inputs may be any that keep to these rules, and one draw needn't show every extreme that they name: Each face_order[i, j, f] is a permutation of 0 to 511. Each krylov_map[i, j] is a permutation of 0 to 1023.
All inputs are finite; a program needn't handle non-finite values.
Results may differ from a plain program's by a relative error of at most 0.0037.
Values sent between devices are 32-bit elements; how exact they have to be, the bound alone decides.
A program may use at most 128 MiB of HBM per device.

v0:
```python
import jax
import jax.numpy as jnp
from jax import lax
from jax.sharding import PartitionSpec as P

BS = 128
FACE = 512
NB = 16
NNZ = 4
SWEEPS = 3
ROWS = 1024
NI = 2048


exact = lax.Precision.HIGHEST


def swapped(block, axis, bit):
    count = lax.axis_size(axis)
    route = []
    for low in range(count):
        high = low | 1 << bit
        if high != low and high < count:
            route += [(low, high), (high, low)]
    return lax.ppermute(block, axis, route)


def eliminate(rhs_cols, offs, dinv, pattern):
    width = rhs_cols.shape[1]
    blocks = rhs_cols.reshape(NB, BS, width)
    picker = (pattern[:, :, None] == jnp.arange(NB, dtype=jnp.int32)[None, None, :]).astype(
        jnp.bfloat16
    )
    picker = picker.reshape(NB * NNZ, NB)
    z_now = jnp.einsum("bij,bjc->bic", dinv, blocks, preferred_element_type=jnp.float32).astype(
        jnp.bfloat16
    )
    for sweep in range(SWEEPS):
        nearby = jnp.dot(picker, z_now.reshape(NB, BS * width), preferred_element_type=jnp.float32)
        nearby = nearby.astype(jnp.bfloat16).reshape(NB, NNZ, BS, width)
        acc = jnp.einsum("bkij,bkjc->bic", offs, nearby, preferred_element_type=jnp.float32)
        resid = (blocks.astype(jnp.float32) - acc).astype(jnp.bfloat16)
        z_now = jnp.einsum("bij,bjc->bic", dinv, resid, preferred_element_type=jnp.float32).astype(
            jnp.bfloat16
        )
    return z_now.reshape(NI, width)


def perm_matrix(order, count):
    return (order[:, None] == jnp.arange(count, dtype=jnp.int32)[None, :]).astype(jnp.float32)


def to_shared(block, order):
    picker = perm_matrix(order, FACE)
    left = jnp.dot(picker, block, precision=exact, preferred_element_type=jnp.float32)
    return jnp.dot(left, picker.T, precision=exact, preferred_element_type=jnp.float32)


def to_local(block, order):
    picker = perm_matrix(order, FACE)
    left = jnp.dot(picker.T, block, precision=exact, preferred_element_type=jnp.float32)
    return jnp.dot(left, picker, precision=exact, preferred_element_type=jnp.float32)


def assemble_a(block, order):
    partner = swapped(to_shared(block, order), "sx", 0)
    return block + to_local(partner, order)


def assemble_b(block, order):
    partner = swapped(to_shared(block, order), "sy", 0)
    return block + to_local(partner, order)


def place_rows(tile, target):
    placer = perm_matrix(target, ROWS).T
    return jnp.dot(placer, tile, precision=exact, preferred_element_type=jnp.float32)


def send_left(new_a, left_cols, target):
    half = jnp.concatenate([new_a, left_cols[FACE:]], axis=0)
    return lax.all_to_all(place_rows(half, target), "sy", split_axis=0, concat_axis=0, tiled=True)


def send_right(new_b, right_cols, target):
    half = jnp.concatenate([right_cols[:FACE], new_b], axis=0)
    return lax.all_to_all(place_rows(half, target), "sy", split_axis=0, concat_axis=0, tiled=True)


def local(
    interior_rhs,
    interface_coupling,
    interface_local,
    off_blocks,
    diag_inverse,
    block_pattern,
    face_order,
    krylov_map,
):
    rhs = interior_rhs[0, 0]
    coupling = interface_coupling[0, 0]
    own = interface_local[0, 0]
    offs = off_blocks[0, 0]
    dinv = diag_inverse[0, 0]
    pattern = block_pattern[0, 0]
    orders = face_order[0, 0]
    target = krylov_map[0, 0]
    moved_left = None
    moved_right = None
    z_all = eliminate(rhs, offs, dinv, pattern)
    schur = own - jnp.dot(coupling, z_all, preferred_element_type=jnp.float32)
    left_cols = schur[:, :FACE]
    right_cols = schur[:, FACE:]
    new_a = assemble_a(left_cols[:FACE], orders[0])
    new_b = assemble_b(right_cols[FACE:], orders[1])
    moved_left = send_left(new_a, left_cols, target)
    moved_right = send_right(new_b, right_cols, target)
    moved = jnp.concatenate([moved_left, moved_right], axis=1)
    return moved[None, None]


def solution(mesh):
    return jax.shard_map(
        local,
        mesh=mesh,
        in_specs=(
            P("sx", "sy", None, None),
            P("sx", "sy", None, None),
            P("sx", "sy", None, None),
            P("sx", "sy", None, None, None, None),
            P("sx", "sy", None, None, None),
            P("sx", "sy", None, None),
            P("sx", "sy", None, None),
            P("sx", "sy", None),
        ),
        out_specs=P("sx", "sy", None, None),
        check_vma=False,
    )
```

profile of v0, /device:TPU:0, one launch (start us, length us, event | category | flops | bytes accessed | tf_op | source)
XLA Modules:
  0.0 297.6 jit_solution(10937994373218653717)
XLA Ops:
  0.0 3.7 %convolution_convert_fusion.3 = bf16[16,128,1024]{2,1,0:T(8,128)(2,1)S(1)} fusion(bf16[16,128,1024]{2,1,0:T(8,128)(2,1)} %bitcast.108, bf16[1,1,16,128,128]{4,3,2,1,0:T(8,128)(2,1)} %param.12), kind=kOutput, calls=%fused_computation.25 | convolution fusion | flops 538968064 | bytes 8912896 | tf_op jit(solution)/shard_map/bij,bjc->bic/dot_general | solution.py:35
  3.8 4.3 %copy.22 = bf16[2,8,128,1024]{3,1,2,0:T(8,128)(2,1)} copy(bf16[2,8,128,1024]{3,2,1,0:T(8,128)(2,1)S(1)} %bitcast.112) | data formatting | bytes 8388608
  8.3 10.8 %convolution_convert_fusion.2 = bf16[64,131072]{1,0:T(8,128)(2,1)} fusion(bf16[16,131072]{1,0:T(8,128)(2,1)} %bitcast.113, s32[64]{0:T(128)S(1)} %eq.37), kind=kOutput, calls=%fused_computation.2 | convolution fusion | flops 276825088 | bytes 20971776 | tf_op jit(solution)/shard_map/dot_general | solution.py:39
  19.1 18.7 %copy.23 = bf16[8,8,128,1024]{3,2,1,0:T(8,128)(2,1)} copy(bf16[8,8,128,1024]{3,1,2,0:T(8,128)(2,1)} %bitcast.103) | data formatting | bytes 33554432
  37.8 10.5 %convert_bitcast_fusion.1 = bf16[16,128,1024]{1,2,0:T(8,128)(2,1)} fusion(bf16[16,128,1024]{2,1,0:T(8,128)(2,1)} %bitcast.109, bf16[16,4,128,1024]{3,2,1,0:T(8,128)(2,1)} %bitcast.104, bf16[1,1,16,4,128,128]{5,4,3,2,1,0:T(8,128)(2,1)S(1)} %copy-done, bf16[1,1,16,128,128]{4,3,2,1,0:T(8,128)(2,1)S(1)} %copy-done.2), kind=kOutput, calls=%fused_computation.20 | convolution fusion | flops 2692743168 | bytes 27787264 | tf_op jit(solution)/shard_map/bij,bjc->bic/dot_general | solution.py:43
  48.3 6.8 %copy.24 = bf16[2,8,128,1024]{3,1,2,0:T(8,128)(2,1)} copy(bf16[2,8,128,1024]{2,3,1,0:T(8,128)(2,1)} %bitcast.115) | data formatting | bytes 8388608
  55.1 10.3 %convolution_convert_fusion.1 = bf16[64,131072]{1,0:T(8,128)(2,1)} fusion(bf16[16,131072]{1,0:T(8,128)(2,1)} %bitcast.116, s32[64]{0:T(128)S(1)} %eq.37), kind=kOutput, calls=%fused_computation.1 | convolution fusion | flops 276825088 | bytes 20971776 | tf_op jit(solution)/shard_map/dot_general | solution.py:39
  65.4 18.6 %copy.25 = bf16[8,8,128,1024]{3,2,1,0:T(8,128)(2,1)} copy(bf16[8,8,128,1024]{3,1,2,0:T(8,128)(2,1)} %bitcast.105) | data formatting | bytes 33554432
  84.0 10.6 %convert_bitcast_fusion = bf16[16,128,1024]{1,2,0:T(8,128)(2,1)} fusion(bf16[16,128,1024]{2,1,0:T(8,128)(2,1)} %bitcast.110, bf16[16,4,128,1024]{3,2,1,0:T(8,128)(2,1)} %bitcast.106, bf16[1,1,16,4,128,128]{5,4,3,2,1,0:T(8,128)(2,1)S(1)} %copy-done, bf16[1,1,16,128,128]{4,3,2,1,0:T(8,128)(2,1)S(1)} %copy-done.2), kind=kOutput, calls=%fused_computation.19 | convolution fusion | flops 2692743168 | bytes 27787264 | tf_op jit(solution)/shard_map/bij,bjc->bic/dot_general | solution.py:43
  94.6 6.8 %copy.26 = bf16[2,8,128,1024]{3,1,2,0:T(8,128)(2,1)} copy(bf16[2,8,128,1024]{2,3,1,0:T(8,128)(2,1)} %bitcast.117) | data formatting | bytes 8388608
  101.5 10.3 %convolution_convert_fusion = bf16[64,131072]{1,0:T(8,128)(2,1)} fusion(bf16[16,131072]{1,0:T(8,128)(2,1)} %bitcast.114, s32[64]{0:T(128)S(1)} %eq.37), kind=kOutput, calls=%fused_computation | convolution fusion | flops 276825088 | bytes 20971776 | tf_op jit(solution)/shard_map/dot_general | solution.py:39
  111.8 18.6 %copy.27 = bf16[8,8,128,1024]{3,2,1,0:T(8,128)(2,1)} copy(bf16[8,8,128,1024]{3,1,2,0:T(8,128)(2,1)} %bitcast.102) | data formatting | bytes 33554432
  130.4 10.6 %fusion.23 = bf16[16,1024,128]{1,2,0:T(8,128)(2,1)} fusion(bf16[16,128,1024]{2,1,0:T(8,128)(2,1)} %bitcast.111, bf16[16,4,128,1024]{3,2,1,0:T(8,128)(2,1)} %bitcast.107, bf16[1,1,16,4,128,128]{5,4,3,2,1,0:T(8,128)(2,1)S(1)} %copy-done, bf16[1,1,16,128,128]{4,3,2,1,0:T(8,128)(2,1)S(1)} %copy-done.2), kind=kOutput, calls=%fused_computation.24 | convolution fusion | flops 2692743168 | bytes 27787264 | tf_op jit(solution)/shard_map/bij,bjc->bic/dot_general | solution.py:43
  141.1 9.1 %bitcast_subtract_fusion = f32[1024,1024]{1,0:T(8,128)S(1)} fusion(f32[1,1,1024,1024]{3,2,1,0:T(8,128)} %param.10, bf16[2048,1024]{1,0:T(8,128)(2,1)} %bitcast.119, bf16[1,1,1024,2048]{3,2,1,0:T(8,128)(2,1)} %param.9), kind=kOutput, calls=%fused_computation.16 | convolution fusion | flops 4296015872 | bytes 16777216 | tf_op jit(solution)/shard_map/dot_general | solution.py:111
  152.5 3.0 %collective-permute-start = (f32[512,512]{1,0:T(8,128)S(1)}, f32[512,512]{1,0:T(8,128)S(1)}, u32[]{:S(2)}, u32[]{:S(2)}) collective-permute-start(f32[512,512]{1,0:T(8,128)S(1)} %fusion.46), channel_id=1, source_target_pairs={{0,8},{8,0},{16,24},{24,16},{1,9},{9,1},{17,25},{25,17},{2,10},{10... | collective-permute-start | bytes 3145736 | tf_op jit(solution)/shard_map/ppermute | solution.py:25
  155.7 23.0 %collective-permute-done = f32[512,512]{1,0:T(8,128)S(1)} collective-permute-done((f32[512,512]{1,0:T(8,128)S(1)}, f32[512,512]{1,0:T(8,128)S(1)}, u32[]{:S(2)}, u32[]{:S(2)}) %collective-permute-start) | collective-permute-done | bytes 1048608 | tf_op jit(solution)/shard_map/ppermute | solution.py:25
  181.1 5.1 %fusion.18 = f32[1024,512]{1,0:T(8,128)} fusion(f32[512,512]{1,0:T(8,128)S(1)} %get-tuple-element.5, f32[512,512]{1,0:T(8,128)S(1)} %convolution_add_fusion.1, s32[1024]{0:T(1024)S(1)} %bitcast.130), kind=kOutput, calls=%fused_computation.23 | convolution fusion | flops 6444023808 | bytes 4198400 | tf_op jit(solution)/shard_map/dot_general | solution.py:77
  186.2 5.4 %all-to-all-start = ((f32[8,128,512]{2,1,0:T(8,128)}), f32[8,128,512]{2,1,0:T(8,128)}, u32[]{:S(2)}, u32[]{:S(2)}) async-start(f32[8,128,512]{2,1,0:T(8,128)} %bitcast.120), calls=%async_computation | async-start | bytes 4194304 | tf_op jit(solution)/shard_map/all_to_all | solution.py:82
  191.6 2.4 fusion.44
  199.2 2.4 convolution_add_fusion
  201.6 5.1 %fusion.17 = f32[1024,512]{1,0:T(8,128)} fusion(f32[512,512]{1,0:T(8,128)S(1)} %convolution_add_fusion, f32[512,512]{1,0:T(8,128)S(1)} %get-tuple-element.6, s32[1024]{0:T(1024)S(1)} %bitcast.131), kind=kOutput, calls=%fused_computation.22 | convolution fusion | flops 6444023808 | bytes 4198400 | tf_op jit(solution)/shard_map/dot_general | solution.py:77
  206.7 34.0 %all-to-all-done = f32[8,128,512]{2,1,0:T(8,128)} async-done(((f32[8,128,512]{2,1,0:T(8,128)}), f32[8,128,512]{2,1,0:T(8,128)}, u32[]{:S(2)}, u32[]{:S(2)}) %all-to-all-start) | async-done | bytes 2097184 | tf_op jit(solution)/shard_map/all_to_all | solution.py:82
  240.7 52.6 %all_to_all.24 = f32[8,128,512]{2,1,0:T(8,128)S(1)} all-to-all(f32[8,128,512]{2,1,0:T(8,128)} %bitcast.121), channel_id=1, replica_groups=mesh['sx'=4,'sy'=8] {'sy'}, dimensions={0} | all-to-all | bytes 4194304 | tf_op jit(solution)/shard_map/all_to_all | solution.py:87
  293.3 4.0 %maximum_bitcast_fusion = f32[1,1,1024,1024]{3,2,1,0:T(8,128)} fusion(f32[1024,512]{1,0:T(8,128)S(1)} %bitcast.118, f32[1024,512]{1,0:T(8,128)} %bitcast.22), kind=kLoop, calls=%fused_computation.15 | loop fusion | flops 1048576 | bytes 8388608 | tf_op jit(solution)/shard_map/broadcast_in_dim | solution.py:119
  (24 shorter events, 10.2 us)
Async XLA Ops:
  0.0 37.8 %copy-start = (bf16[1,1,16,4,128,128]{5,4,3,2,1,0:T(8,128)(2,1)S(1)}, bf16[1,1,16,4,128,128]{5,4,3,2,1,0:T(8,128)(2,1)}, u32[]{:S(2)}) copy-start(bf16[1,1,16,4,128,128]{5,4,3,2,1,0:T(8,128)(2,1)} %param.11) | copy-start | bytes 6291460
  3.7 4.4 %copy-start.4 = (s32[1,1,16,4]{2,3,1,0:T(4,128)S(1)}, s32[1,1,16,4]{2,3,1,0:T(4,128)}, u32[]{:S(2)}) copy-start(s32[1,1,16,4]{2,3,1,0:T(4,128)} %param.13) | copy-start | bytes 772
  19.1 18.7 %copy-start.2 = (bf16[1,1,16,128,128]{4,3,2,1,0:T(8,128)(2,1)S(1)}, bf16[1,1,16,128,128]{4,3,2,1,0:T(8,128)(2,1)}, u32[]{:S(2)}) copy-start(bf16[1,1,16,128,128]{4,3,2,1,0:T(8,128)(2,1)} %param.12) | copy-start | bytes 1572868
  130.4 10.7 %copy-start.3 = (s32[1,1,2,512]{3,2,1,0:T(2,128)S(1)}, s32[1,1,2,512]{3,2,1,0:T(2,128)}, u32[]{:S(2)}) copy-start(s32[1,1,2,512]{3,2,1,0:T(2,128)} %param.14) | copy-start | bytes 12292
  150.2 29.7 %copy-start.1 = (f32[1024,1024]{1,0:T(8,128)}, f32[1024,1024]{1,0:T(8,128)S(1)}, u32[]{:S(2)}) copy-start(f32[1024,1024]{1,0:T(8,128)S(1)} %bitcast_subtract_fusion) | copy-start | bytes 12582916
  152.5 28.6 %copy-start.5 = (s32[1,1,1024]{2,1,0:T(1,128)S(1)}, s32[1,1,1024]{2,1,0:T(1,128)}, u32[]{:S(2)}) copy-start(s32[1,1,1024]{2,1,0:T(1,128)} %param.15) | copy-start | bytes 12292
  152.5 26.2 %collective-permute-start = (f32[512,512]{1,0:T(8,128)S(1)}, f32[512,512]{1,0:T(8,128)S(1)}, u32[]{:S(2)}, u32[]{:S(2)}) collective-permute-start(f32[512,512]{1,0:T(8,128)S(1)} %fusion.46), channel_id=1, source_target_pairs={{0,8},{8,0},{16,24},{24,16},{1,9},{9,1},{17,25},{25,17},{2,10},{10... | collective-permute-start | bytes 3145736 | tf_op jit(solution)/shard_map/ppermute | solution.py:25
  186.2 54.5 %all-to-all-start = ((f32[8,128,512]{2,1,0:T(8,128)}), f32[8,128,512]{2,1,0:T(8,128)}, u32[]{:S(2)}, u32[]{:S(2)}) async-start(f32[8,128,512]{2,1,0:T(8,128)} %bitcast.120), calls=%async_computation | async-start | bytes 4194304 | tf_op jit(solution)/shard_map/all_to_all | solution.py:82
  195.2 2.9 collective-permute-start.1
where the time goes:
time: 302 us; the launch traced here: 298 us
  matrix products  98 us (32%)
  local copies, waits for them, and re-layouts  74.3 us (25%)
  waiting for transfers between devices  59.3 us (20%)
  blocking collectives  52.6 us (17%)
  starting transfers between devices  9.01 us (3%)
  other arithmetic  4.05 us (1%)
    unnamed x19, local copies, waits for them, and re-layouts  74 us
    all_to_all x1, blocking collectives, send_right(): lax.all_to_all(place_rows(half, target), 'sy', split_axis=0, concat_axis=...  52.6 us
    all_to_all x1, waiting for transfers between devices, send_left(): lax.all_to_all(place_rows(half, target), 'sy', split_axis=0, concat_axis=...  34 us
    dot_general x3, matrix products, eliminate(): jnp.einsum('bij,bjc->bic', dinv, resid, preferred_element_type=jnp.float32)  31.7 us
    dot_general x3, matrix products, eliminate(): jnp.dot(picker, z_now.reshape(NB, BS * width), preferred_element_type=jnp...  31.4 us
    ppermute x2, waiting for transfers between devices, swapped(): return lax.ppermute(block, axis, route)  25.3 us
    dot_general x2, matrix products, place_rows(): jnp.dot(placer, tile, precision=exact, preferred_element_type=jnp.float32)  10.2 us
    dot_general x1, matrix products, local(): schur = own - jnp.dot(coupling, z_all, preferred_element_type=jnp.float32)  9.15 us
  transfers between devices with their start and end apart: 3, of which 3 were waited for; matrix products, arithmetic and copies ran while one was open for 4% of the time, Pallas kernels for 0%

commit v1 on v0

v1 whole, which is shorter than its diff:
```python
import functools

import jax
import jax.numpy as jnp
from jax import lax
from jax.experimental import pallas as pl
from jax.experimental.pallas import tpu as pltpu
from jax.sharding import PartitionSpec as P

SWEEPS = 3
GROUP = 4
F32 = jnp.float32
BF16 = jnp.bfloat16
VMEM_LIMIT = 50 * 2**20


def swapped(block, axis):
    count = lax.axis_size(axis)
    route = []
    for low in range(count):
        high = low | 1
        if high != low and high < count:
            route += [(low, high), (high, low)]
    return lax.ppermute(block, axis, route)


def dot(a, b):
    return jnp.dot(a, b, preferred_element_type=F32)


def halves(values):
    high = values.astype(BF16)
    return high, (values - high.astype(F32)).astype(BF16)


def picker_of(col, count):
    spot = lax.broadcasted_iota(jnp.int32, (col.shape[0], count), 1)
    return jnp.where(spot == col, F32(1), F32(0)).astype(BF16)


def picker_t_of(row, count, first=0):
    spot = lax.broadcasted_iota(jnp.int32, (count, row.shape[1]), 0) + first
    return jnp.where(spot == row, F32(1), F32(0)).astype(BF16)


def both_sides(left, block, right):
    high, low = halves(block)
    return dot(dot(left, high).astype(BF16), right) + dot(dot(left, low).astype(BF16), right)


def eliminate_kernel(
    side, pattern, rhs_hbm, offs_hbm, dinv_hbm, coupling_hbm, own_hbm, col_ref, row_ref,
    schur, shared, rhs, offs, dinv, coupling, own, z, sems,
):
    blocks, size, width = rhs.shape
    nnz = offs.shape[1]
    face = row_ref.shape[1]
    cols = pl.ds(side * width, width)
    moves = [
        pltpu.make_async_copy(dinv_hbm, dinv, sems.at[0]),
        pltpu.make_async_copy(rhs_hbm.at[:, :, cols], rhs, sems.at[1]),
        pltpu.make_async_copy(offs_hbm, offs, sems.at[2]),
        pltpu.make_async_copy(coupling_hbm, coupling, sems.at[3]),
        pltpu.make_async_copy(own_hbm.at[:, cols], own, sems.at[4]),
    ]
    for move in moves:
        move.start()
    moves[0].wait()
    moves[1].wait()

    @pl.loop(0, blocks // GROUP)
    def _(group):
        for part in range(GROUP):
            b = group * GROUP + part
            z[0, b] = dot(dinv[b], rhs[b]).astype(BF16)

    moves[2].wait()
    for sweep in range(SWEEPS):
        old, new = sweep % 2, (sweep + 1) % 2

        @pl.loop(0, blocks // GROUP)
        def _(group):
            for part in range(GROUP):
                b = group * GROUP + part
                row = jnp.concatenate([offs[b, k] for k in range(nnz)], axis=1)
                near = jnp.concatenate([z[old, pattern[b, k]] for k in range(nnz)], axis=0)
                resid = (rhs[b].astype(F32) - dot(row, near)).astype(BF16)
                z[new, b] = dot(dinv[b], resid).astype(BF16)

    moves[3].wait()
    moves[4].wait()
    rows = own.shape[0]
    tile = rows // 4

    @pl.loop(0, 4)
    def _(step):
        span = pl.ds(pl.multiple_of(step * tile, tile), tile)
        done = z[SWEEPS % 2].reshape(blocks * size, width)
        schur[span, :] = own[span, :] - dot(coupling[span, :], done)

    left = picker_of(col_ref[...], face)
    right = picker_t_of(row_ref[...], face)
    shared[...] = both_sides(left, schur[pl.ds(side * face, face), :], right)


def eliminate(side, pattern, rhs, offs, dinv, coupling, own, col, row):
    blocks, size, all_cols = rhs.shape
    face = row.shape[1]
    rows = own.shape[0]
    width = all_cols // 2
    macs = blocks * size * width * size * (1 + SWEEPS * (1 + offs.shape[1])) + rows * blocks * size * width
    anywhere = pl.BlockSpec(memory_space=pl.ANY)
    vmem = pl.BlockSpec(memory_space=pltpu.VMEM)
    return pl.pallas_call(
        functools.partial(eliminate_kernel, side),
        out_shape=(
            jax.ShapeDtypeStruct((rows, width), F32),
            jax.ShapeDtypeStruct((face, face), F32),
        ),
        in_specs=[pl.BlockSpec(memory_space=pltpu.SMEM)] + [anywhere] * 5 + [vmem] * 2,
        out_specs=(vmem, vmem),
        scratch_shapes=[
            pltpu.VMEM((blocks, size, width), BF16),
            pltpu.VMEM(offs.shape, BF16),
            pltpu.VMEM(dinv.shape, BF16),
            pltpu.VMEM(coupling.shape, BF16),
            pltpu.VMEM((rows, width), F32),
            pltpu.VMEM((2, blocks, size, width), BF16),
            pltpu.SemaphoreType.DMA((5,)),
        ],
        compiler_params=pltpu.CompilerParams(vmem_limit_bytes=VMEM_LIMIT),
        cost_estimate=pl.CostEstimate(flops=4 * macs, bytes_accessed=12 * 2**20, transcendentals=0),
    )(pattern, rhs, offs, dinv, coupling, own, col, row)


def place_kernel(side, schur, got, col_ref, row_ref, target_ref, placed, high, low):
    face = row_ref.shape[1]
    rows = schur.shape[0]
    mine = pl.ds(side * face, face)
    rest = pl.ds((1 - side) * face, face)
    high[rest, :], low[rest, :] = halves(schur[rest, :])
    back = both_sides(picker_t_of(row_ref[...], face), got[...], picker_of(col_ref[...], face))
    high[mine, :], low[mine, :] = halves(schur[mine, :] + back)
    tile = rows // 4

    @pl.loop(0, 4)
    def _(step):
        first = pl.multiple_of(step * tile, tile)
        placer = picker_t_of(target_ref[...], tile, first)
        placed[pl.ds(first, tile), :] = dot(placer, high[...]) + dot(placer, low[...])


def place(side, schur, got, col, row, target):
    rows, width = schur.shape
    vmem = pl.BlockSpec(memory_space=pltpu.VMEM)
    return pl.pallas_call(
        functools.partial(place_kernel, side),
        out_shape=jax.ShapeDtypeStruct((rows, width), F32),
        in_specs=[vmem] * 5,
        out_specs=vmem,
        scratch_shapes=[pltpu.VMEM((rows, width), BF16), pltpu.VMEM((rows, width), BF16)],
        compiler_params=pltpu.CompilerParams(vmem_limit_bytes=VMEM_LIMIT),
        cost_estimate=pl.CostEstimate(
            flops=4 * rows * rows * width, bytes_accessed=5 * 2**20, transcendentals=0
        ),
    )(schur, got, col, row, target)


def send(placed):
    return lax.all_to_all(placed, "sy", split_axis=0, concat_axis=0, tiled=True)


def local(
    interior_rhs,
    interface_coupling,
    interface_local,
    off_blocks,
    diag_inverse,
    block_pattern,
    face_order,
    krylov_map,
):
    coupling = interface_coupling[0, 0]
    own = interface_local[0, 0]
    offs = off_blocks[0, 0]
    dinv = diag_inverse[0, 0]
    pattern = block_pattern[0, 0]
    rhs = interior_rhs[0, 0].reshape(dinv.shape[0], dinv.shape[1], own.shape[1])
    orders = face_order[0, 0]
    target = krylov_map[0]
    col = [orders[f][:, None] for f in range(2)]
    row = [orders[f][None, :] for f in range(2)]

    schur_b, shared_b = eliminate(1, pattern, rhs, offs, dinv, coupling, own, col[1], row[1])
    got_b = swapped(shared_b, "sy")
    placed_b = place(1, schur_b, got_b, col[1], row[1], target)
    placed_b, pattern = lax.optimization_barrier((placed_b, pattern))
    moved_b = send(placed_b)
    schur_a, shared_a = eliminate(0, pattern, rhs, offs, dinv, coupling, own, col[0], row[0])
    got_a = swapped(shared_a, "sx")
    placed_a = place(0, schur_a, got_a, col[0], row[0], target)
    moved_a = send(placed_a)
    return jnp.concatenate([moved_a, moved_b], axis=1)[None, None]


def solution(mesh):
    return jax.shard_map(
        local,
        mesh=mesh,
        in_specs=(
            P("sx", "sy", None, None),
            P("sx", "sy", None, None),
            P("sx", "sy", None, None),
            P("sx", "sy", None, None, None, None),
            P("sx", "sy", None, None, None),
            P("sx", "sy", None, None),
            P("sx", "sy", None, None),
            P("sx", "sy", None),
        ),
        out_specs=P("sx", "sy", None, None),
        check_vma=False,
    )
```

time: 302 us -> 165 us (0.55); the launches traced: 298 us -> 165 us
  matrix products: 98 us -> 0 us
  local copies, waits for them, and re-layouts: 74.3 us -> 5.58 us
  Pallas kernels: 0 us -> 66.7 us
  waiting for transfers between devices: 59.3 us -> 26.4 us
    dot_general x18 -> x0, matrix products: 98 us -> none  [the longest x3 31.7 us: eliminate(): jnp.einsum('bij,bjc->bic', dinv, resid, preferred_element_type=jnp.float32)]
    unnamed x19 -> x12, local copies, waits for them, and re-layouts: 74 us -> 3.68 us
    pallas_call x0 -> x4, Pallas kernels: none -> 66.7 us  [the longest x2 53.3 us: eliminate(): pl.pallas_call(functools.partial(eliminate_kernel, side), out_shape=(jax....]
    all_to_all x1, waiting for transfers between devices: 34 us -> 0.01 us  [send(): return lax.all_to_all(placed, 'sy', split_axis=0, concat_axis=0, tiled=True)]
  transfers between devices with their start and end apart: 3 -> 3, of which waited for: 3 -> 2; matrix products, arithmetic and copies ran while one was open for 4% -> 0% of each run, Pallas kernels for 0% -> 20%
where the time goes in v1:
time: 165 us
  Pallas kernels  66.7 us (40%)
  blocking collectives  53.6 us (32%)
  waiting for transfers between devices  26.4 us (16%)
  starting transfers between devices  8.33 us (5%)
  local copies, waits for them, and re-layouts  5.58 us (3%)
  other arithmetic  4.11 us (2%)
    all_to_all x1, blocking collectives, send(): return lax.all_to_all(placed, 'sy', split_axis=0, concat_axis=0, tiled=True)  53.6 us
    pallas_call x2, Pallas kernels, eliminate(): pl.pallas_call(functools.partial(eliminate_kernel, side), out_shape=(jax....  53.3 us
    ppermute x2, waiting for transfers between devices, swapped(): return lax.ppermute(block, axis, route)  26.4 us
    pallas_call x2, Pallas kernels, place(): pl.pallas_call(functools.partial(place_kernel, side), out_shape=jax.Shape...  13.5 us
    all_to_all x1, starting transfers between devices, send(): return lax.all_to_all(placed, 'sy', split_axis=0, concat_axis=0, tiled=True)  6.35 us
    broadcast_in_dim x1, other arithmetic, local(): return jnp.concatenate([moved_a, moved_b], axis=1)[None, None]  4.11 us
    unnamed x12, local copies, waits for them, and re-layouts  3.68 us
  transfers between devices with their start and end apart: 3, of which 2 were waited for; matrix products, arithmetic and copies ran while one was open for 0% of the time, Pallas kernels for 20%

profile of v1, /device:TPU:0, one launch (start us, length us, event | category | flops | bytes accessed | tf_op | source)
XLA Modules:
  0.0 164.8 jit_solution(5839627226792665188)
XLA Ops:
  0.0 0.8 copy.11.pattern
  0.8 0.8 slice_bitcast_fusion
  1.5 0.1 copy.12.col_ref
  1.7 0.0 copy-start
  1.7 1.0 copy-done
  2.7 26.6 %shard_map.82 = (f32[1024,512]{1,0:T(8,128)S(1)}, f32[512,512]{1,0:T(8,128)S(1)}) custom-call(s32[16,4]{1,0:T(8,128)S(1)} %copy.11.pattern, bf16[16,128,1024]{2,1,0:T(8,128)(2,1)} %bitcast.29, bf16[16,4,128,128]{3,2,1,0:T(8,128)(2,1)} %bitcast.35, bf16[16,128,128]{2,1,0:T(8,128)(2,1)S(1)} %bitcast.22, bf16[1024,2048]{1,0:T(8,128)(2,1)} %bitcast.31, ...), custom_call_target="tpu_custom_call" | custom-call | flops 12884901888 | bytes 12582912 | tf_op jit(solution)/shard_map/pallas_call | solution.py:114
  29.4 0.0 copy-start.3
  29.4 1.3 copy-done.3
  30.7 0.5 collective-permute-start
  31.2 2.3 %collective-permute-done.got = f32[512,512]{1,0:T(8,128)S(1)} collective-permute-done((f32[512,512]{1,0:T(8,128)S(1)}, f32[512,512]{1,0:T(8,128)S(1)}, u32[]{:S(2)}, u32[]{:S(2)}) %collective-permute-start) | collective-permute-done | bytes 1048608 | tf_op jit(solution)/shard_map/ppermute | solution.py:24
  33.5 0.0 copy-done.2
  33.5 7.4 %shard_map.83 = f32[1024,512]{1,0:T(8,128)} custom-call(f32[1024,512]{1,0:T(8,128)} %copy-done.3, f32[512,512]{1,0:T(8,128)S(1)} %collective-permute-done.got, s32[512,1]{1,0:T(8,128)S(1)} %copy.12.col_ref, s32[1,512]{1,0:T(1,128)S(1)} %get-tuple-element.18.row_ref, s32[1,1024]{1,0:T(1,128)S(1)} %bitcast.24), custom_call_target="tpu_custom_call" | custom-call | flops 2147483648 | bytes 5242880 | tf_op jit(solution)/shard_map/pallas_call | solution.py:156
  40.9 6.4 %all-to-all-start.1 = ((f32[8,128,512]{2,1,0:T(8,128)}), f32[8,128,512]{2,1,0:T(8,128)}, u32[]{:S(2)}, u32[]{:S(2)}) async-start(f32[8,128,512]{2,1,0:T(8,128)} %bitcast.13), calls=%async_computation.1 | async-start | bytes 4194304 | tf_op jit(solution)/shard_map/all_to_all | solution.py:170
  47.2 0.1 copy.15.col_ref
  47.4 0.1 copy.14.pattern
  47.5 26.6 %shard_map.84 = (f32[1024,512]{1,0:T(8,128)S(1)}, f32[512,512]{1,0:T(8,128)S(1)}) custom-call(s32[16,4]{1,0:T(8,128)S(1)} %copy.14.pattern, bf16[16,128,1024]{2,1,0:T(8,128)(2,1)} %bitcast.30, bf16[16,4,128,128]{3,2,1,0:T(8,128)(2,1)} %bitcast.36, bf16[16,128,128]{2,1,0:T(8,128)(2,1)S(1)} %bitcast.23, bf16[1024,2048]{1,0:T(8,128)(2,1)} %bitcast.32, ...), custom_call_target="tpu_custom_call" | custom-call | flops 12884901888 | bytes 12582912 | tf_op jit(solution)/shard_map/pallas_call | solution.py:114
  74.1 0.0 copy-start.4
  74.1 1.3 copy-done.4
  75.4 1.5 collective-permute-start.1
  76.9 24.1 %collective-permute-done.1.got = f32[512,512]{1,0:T(8,128)S(1)} collective-permute-done((f32[512,512]{1,0:T(8,128)S(1)}, f32[512,512]{1,0:T(8,128)S(1)}, u32[]{:S(2)}, u32[]{:S(2)}) %collective-permute-start.1) | collective-permute-done | bytes 1048608 | tf_op jit(solution)/shard_map/ppermute | solution.py:24
  101.0 6.1 %shard_map.85 = f32[1024,512]{1,0:T(8,128)S(1)} custom-call(f32[1024,512]{1,0:T(8,128)} %copy-done.4, f32[512,512]{1,0:T(8,128)S(1)} %collective-permute-done.1.got, s32[512,1]{1,0:T(8,128)S(1)} %copy.15.col_ref, s32[1,512]{1,0:T(1,128)S(1)} %get-tuple-element.17.row_ref, s32[1,1024]{1,0:T(1,128)S(1)} %bitcast.25), custom_call_target="tpu_custom_call" | custom-call | flops 2147483648 | bytes 5242880 | tf_op jit(solution)/shard_map/pallas_call | solution.py:156
  107.1 0.0 all-to-all-done.1
  107.1 53.6 %all_to_all.24 = f32[8,128,512]{2,1,0:T(8,128)S(1)} all-to-all(f32[8,128,512]{2,1,0:T(8,128)S(1)} %bitcast.21), channel_id=1, replica_groups=mesh['sx'=4,'sy'=8] {'sy'}, dimensions={0} | all-to-all | bytes 4194304 | tf_op jit(solution)/shard_map/all_to_all | solution.py:170
  160.7 4.1 %maximum_bitcast_fusion = f32[1,1,1024,1024]{3,2,1,0:T(8,128)} fusion(f32[1024,512]{1,0:T(8,128)} %bitcast.14, f32[1024,512]{1,0:T(8,128)S(1)} %bitcast.26), kind=kLoop, calls=%fused_computation | loop fusion | flops 1048576 | bytes 8388608 | tf_op jit(solution)/shard_map/broadcast_in_dim | solution.py:203
  (5 shorter events, 0.0 us)
Async XLA Ops:
  1.7 1.0 copy-start
  2.7 30.7 %copy-start.2 = (s32[1,1,1024]{2,1,0:T(1,128)S(1)}, s32[1,1,1024]{2,1,0:T(1,128)}, u32[]{:S(2)}) copy-start(s32[1,1,1024]{2,1,0:T(1,128)} %param.15) | copy-start | bytes 12292
  29.4 1.3 copy-start.3
  30.7 2.8 %collective-permute-start = (f32[512,512]{1,0:T(8,128)S(1)}, f32[512,512]{1,0:T(8,128)S(1)}, u32[]{:S(2)}, u32[]{:S(2)}) collective-permute-start(f32[512,512]{1,0:T(8,128)S(1)} %get-tuple-element.12), channel_id=1, source_target_pairs={{0,1},{1,0},{2,3},{3,2},{4,5},{5,4},{6,7},{7,6},{8,9},{9,8},{10,11... | collective-permute-start | bytes 3145736 | tf_op jit(solution)/shard_map/ppermute | solution.py:24
  40.9 6.5 %copy-start.5 = (s32[1,1,16,4]{2,3,1,0:T(4,128)S(1)}, s32[1,1,16,4]{2,3,1,0:T(4,128)}, u32[]{:S(2)}) copy-start(s32[1,1,16,4]{2,3,1,0:T(4,128)} %param.13) | copy-start | bytes 772
  40.9 6.6 %copy-start.1 = (bf16[1,1,16,128,128]{4,3,2,1,0:T(8,128)(2,1)S(1)}, bf16[1,1,16,128,128]{4,3,2,1,0:T(8,128)(2,1)}, u32[]{:S(2)}) copy-start(bf16[1,1,16,128,128]{4,3,2,1,0:T(8,128)(2,1)} %param.12) | copy-start | bytes 1572868
  40.9 66.2 %all-to-all-start.1 = ((f32[8,128,512]{2,1,0:T(8,128)}), f32[8,128,512]{2,1,0:T(8,128)}, u32[]{:S(2)}, u32[]{:S(2)}) async-start(f32[8,128,512]{2,1,0:T(8,128)} %bitcast.13), calls=%async_computation.1 | async-start | bytes 4194304 | tf_op jit(solution)/shard_map/all_to_all | solution.py:170
  74.1 1.3 copy-start.4
  75.4 25.6 %collective-permute-start.1 = (f32[512,512]{1,0:T(8,128)S(1)}, f32[512,512]{1,0:T(8,128)S(1)}, u32[]{:S(2)}, u32[]{:S(2)}) collective-permute-start(f32[512,512]{1,0:T(8,128)S(1)} %get-tuple-element.15), channel_id=1, source_target_pairs={{0,8},{8,0},{16,24},{24,16},{1,9},{9,1},{17,25},{25,17},{2,10},{10... | collective-permute-start | bytes 3145736 | tf_op jit(solution)/shard_map/ppermute | solution.py:24

commit v2 on v1

--- a/solution.py
+++ b/solution.py
@@ -8,10 +8,13 @@
 from jax.sharding import PartitionSpec as P
 
 SWEEPS = 3
-GROUP = 4
+GROUP = 16
+PAIR = 4
+TILES = 2
 F32 = jnp.float32
 BF16 = jnp.bfloat16
 VMEM_LIMIT = 50 * 2**20
+PLACE_LIMIT = 18 * 2**20
 
 
 def swapped(block, axis):
@@ -50,7 +53,7 @@
 
 def eliminate_kernel(
     side, pattern, rhs_hbm, offs_hbm, dinv_hbm, coupling_hbm, own_hbm, col_ref, row_ref,
-    schur, shared, rhs, offs, dinv, coupling, own, z, sems,
+    schur, shared, rhs, offs, dinv, coupling, own, even, odd, sems,
 ):
     blocks, size, width = rhs.shape
     nnz = offs.shape[1]
@@ -72,30 +75,35 @@
     def _(group):
         for part in range(GROUP):
             b = group * GROUP + part
-            z[0, b] = dot(dinv[b], rhs[b]).astype(BF16)
+            even[b] = dot(dinv[b], rhs[b]).astype(BF16)
 
     moves[2].wait()
     for sweep in range(SWEEPS):
-        old, new = sweep % 2, (sweep + 1) % 2
+        old, new = ((even, odd), (odd, even))[sweep % 2]
 
         @pl.loop(0, blocks // GROUP)
         def _(group):
+            resid = []
             for part in range(GROUP):
                 b = group * GROUP + part
                 row = jnp.concatenate([offs[b, k] for k in range(nnz)], axis=1)
-                near = jnp.concatenate([z[old, pattern[b, k]] for k in range(nnz)], axis=0)
-                resid = (rhs[b].astype(F32) - dot(row, near)).astype(BF16)
-                z[new, b] = dot(dinv[b], resid).astype(BF16)
+                near = jnp.concatenate([old[pattern[b, k]] for k in range(nnz)], axis=0)
+                resid.append((rhs[b].astype(F32) - dot(row, near)).astype(BF16))
+                if part % PAIR == PAIR - 1:
+                    for late in range(part - PAIR + 1, part + 1):
+                        spot = group * GROUP + late
+                        new[spot] = dot(dinv[spot], resid[late]).astype(BF16)
 
     moves[3].wait()
     moves[4].wait()
     rows = own.shape[0]
-    tile = rows // 4
-
-    @pl.loop(0, 4)
+    tile = rows // TILES
+    last = (even, odd)[SWEEPS % 2]
+
+    @pl.loop(0, TILES)
     def _(step):
         span = pl.ds(pl.multiple_of(step * tile, tile), tile)
-        done = z[SWEEPS % 2].reshape(blocks * size, width)
+        done = last[...].reshape(blocks * size, width)
         schur[span, :] = own[span, :] - dot(coupling[span, :], done)
 
     left = picker_of(col_ref[...], face)
@@ -125,7 +133,8 @@
             pltpu.VMEM(dinv.shape, BF16),
             pltpu.VMEM(coupling.shape, BF16),
             pltpu.VMEM((rows, width), F32),
-            pltpu.VMEM((2, blocks, size, width), BF16),
+            pltpu.VMEM((blocks, size, width), BF16),
+            pltpu.VMEM((blocks, size, width), BF16),
             pltpu.SemaphoreType.DMA((5,)),
         ],
         compiler_params=pltpu.CompilerParams(vmem_limit_bytes=VMEM_LIMIT),
@@ -159,7 +168,7 @@
         in_specs=[vmem] * 5,
         out_specs=vmem,
         scratch_shapes=[pltpu.VMEM((rows, width), BF16), pltpu.VMEM((rows, width), BF16)],
-        compiler_params=pltpu.CompilerParams(vmem_limit_bytes=VMEM_LIMIT),
+        compiler_params=pltpu.CompilerParams(vmem_limit_bytes=PLACE_LIMIT),
         cost_estimate=pl.CostEstimate(
             flops=4 * rows * rows * width, bytes_accessed=5 * 2**20, transcendentals=0
         ),

time: 165 us -> 136 us (0.82)
  Pallas kernels: 66.7 us -> 35.6 us
  waiting for transfers between devices: 26.4 us -> 32.5 us
  local copies, waits for them, and re-layouts: 5.58 us -> 2.95 us
  blocking collectives: 53.6 us -> 51.5 us
    pallas_call x2, Pallas kernels: 53.3 us -> 25.4 us  [eliminate(): pl.pallas_call(functools.partial(eliminate_kernel, side), out_shape=(jax....]
    all_to_all x1, waiting for transfers between devices: 0.01 us -> 6.16 us  [send(): return lax.all_to_all(placed, 'sy', split_axis=0, concat_axis=0, tiled=True)]
    pallas_call x2, Pallas kernels: 13.5 us -> 10.2 us  [place(): pl.pallas_call(functools.partial(place_kernel, side), out_shape=jax.Shape...]
    unnamed x12 -> x8, local copies, waits for them, and re-layouts: 3.68 us -> 1.05 us
    all_to_all x1, blocking collectives: 53.6 us -> 51.5 us  [send(): return lax.all_to_all(placed, 'sy', split_axis=0, concat_axis=0, tiled=True)]
  transfers between devices with their start and end apart: 3 -> 3, of which waited for: 2 -> 3; matrix products, arithmetic and copies ran while one was open for 0% -> 0% of each run, Pallas kernels for 20% -> 13%
where the time goes in v2:
time: 136 us; the launch traced here: 135 us
  blocking collectives  51.5 us (38%)
  Pallas kernels  35.6 us (26%)
  waiting for transfers between devices  32.5 us (24%)
  starting transfers between devices  8.47 us (6%)
  other arithmetic  4.11 us (3%)
  local copies, waits for them, and re-layouts  2.95 us (2%)
    all_to_all x1, blocking collectives, send(): return lax.all_to_all(placed, 'sy', split_axis=0, concat_axis=0, tiled=True)  51.5 us
    ppermute x2, waiting for transfers between devices, swapped(): return lax.ppermute(block, axis, route)  26.4 us
    pallas_call x2, Pallas kernels, eliminate(): pl.pallas_call(functools.partial(eliminate_kernel, side), out_shape=(jax....  25.4 us
    pallas_call x2, Pallas kernels, place(): pl.pallas_call(functools.partial(place_kernel, side), out_shape=jax.Shape...  10.2 us
    all_to_all x1, starting transfers between devices, send(): return lax.all_to_all(placed, 'sy', split_axis=0, concat_axis=0, tiled=True)  6.4 us
    all_to_all x1, waiting for transfers between devices, send(): return lax.all_to_all(placed, 'sy', split_axis=0, concat_axis=0, tiled=True)  6.16 us
    broadcast_in_dim x1, other arithmetic, local(): return jnp.concatenate([moved_a, moved_b], axis=1)[None, None]  4.11 us
  transfers between devices with their start and end apart: 3, of which 3 were waited for; matrix products, arithmetic and copies ran while one was open for 0% of the time, Pallas kernels for 13%

profile of v2, /device:TPU:0, one launch (start us, length us, event | category | flops | bytes accessed | tf_op | source)
XLA Modules:
  0.0 135.2 jit_solution(17333160442186334219)
XLA Ops:
  0.0 0.8 copy.11.pattern
  0.8 0.8 slice_bitcast_fusion
  1.5 0.1 copy.12.col_ref
  1.7 0.0 copy-start
  1.7 1.0 copy-done
  2.7 0.0 copy-start.2
  2.7 12.7 %shard_map.82 = (f32[1024,512]{1,0:T(8,128)S(1)}, f32[512,512]{1,0:T(8,128)S(1)}) custom-call(s32[16,4]{1,0:T(8,128)S(1)} %copy.11.pattern, bf16[16,128,1024]{2,1,0:T(8,128)(2,1)} %bitcast.29, bf16[16,4,128,128]{3,2,1,0:T(8,128)(2,1)} %bitcast.35, bf16[16,128,128]{2,1,0:T(8,128)(2,1)S(1)} %bitcast.22, bf16[1024,2048]{1,0:T(8,128)(2,1)} %bitcast.31, ...), custom_call_target="tpu_custom_call" | custom-call | flops 12884901888 | bytes 12582912 | tf_op jit(solution)/shard_map/pallas_call | solution.py:122
  15.4 0.5 collective-permute-start
  16.0 2.3 %collective-permute-done.got = f32[512,512]{1,0:T(8,128)S(1)} collective-permute-done((f32[512,512]{1,0:T(8,128)S(1)}, f32[512,512]{1,0:T(8,128)S(1)}, u32[]{:S(2)}, u32[]{:S(2)}) %collective-permute-start) | collective-permute-done | bytes 1048608 | tf_op jit(solution)/shard_map/ppermute | solution.py:27
  18.2 0.0 copy-done.2
  18.2 5.8 %shard_map.83 = f32[1024,512]{1,0:T(8,128)} custom-call(f32[1024,512]{1,0:T(8,128)S(1)} %get-tuple-element.11.schur, f32[512,512]{1,0:T(8,128)S(1)} %collective-permute-done.got, s32[512,1]{1,0:T(8,128)S(1)} %copy.12.col_ref, s32[1,512]{1,0:T(1,128)S(1)} %get-tuple-element.18.row_ref, s32[1,1024]{1,0:T(1,128)S(1)} %bitcast.24), custom_call_target="tpu_custom_call" | custom-call | flops 2147483648 | bytes 5242880 | tf_op jit(solution)/shard_map/pallas_call | solution.py:165
  24.0 0.0 copy-start.3
  24.0 6.4 %all-to-all-start.1 = ((f32[8,128,512]{2,1,0:T(8,128)}), f32[8,128,512]{2,1,0:T(8,128)}, u32[]{:S(2)}, u32[]{:S(2)}) async-start(f32[8,128,512]{2,1,0:T(8,128)} %bitcast.13), calls=%async_computation.1 | async-start | bytes 4194304 | tf_op jit(solution)/shard_map/all_to_all | solution.py:179
  30.4 0.1 copy.15.col_ref
  30.6 0.0 copy-done.3
  30.6 0.1 copy.14.pattern
  30.7 0.0 copy-done.1
  30.7 12.7 %shard_map.84 = (f32[1024,512]{1,0:T(8,128)S(1)}, f32[512,512]{1,0:T(8,128)S(1)}) custom-call(s32[16,4]{1,0:T(8,128)S(1)} %copy.14.pattern, bf16[16,128,1024]{2,1,0:T(8,128)(2,1)} %bitcast.30, bf16[16,4,128,128]{3,2,1,0:T(8,128)(2,1)} %bitcast.36, bf16[16,128,128]{2,1,0:T(8,128)(2,1)S(1)} %bitcast.23, bf16[1024,2048]{1,0:T(8,128)(2,1)} %bitcast.32, ...), custom_call_target="tpu_custom_call" | custom-call | flops 12884901888 | bytes 12582912 | tf_op jit(solution)/shard_map/pallas_call | solution.py:122
  43.4 1.5 %collective-permute-start.1 = (f32[512,512]{1,0:T(8,128)S(1)}, f32[512,512]{1,0:T(8,128)S(1)}, u32[]{:S(2)}, u32[]{:S(2)}) collective-permute-start(f32[512,512]{1,0:T(8,128)S(1)} %get-tuple-element.15), channel_id=1, source_target_pairs={{0,8},{8,0},{16,24},{24,16},{1,9},{9,1},{17,25},{25,17},{2,10},{10... | collective-permute-start | bytes 3145736 | tf_op jit(solution)/shard_map/ppermute | solution.py:27
  44.9 24.1 %collective-permute-done.1.got = f32[512,512]{1,0:T(8,128)S(1)} collective-permute-done((f32[512,512]{1,0:T(8,128)S(1)}, f32[512,512]{1,0:T(8,128)S(1)}, u32[]{:S(2)}, u32[]{:S(2)}) %collective-permute-start.1) | collective-permute-done | bytes 1048608 | tf_op jit(solution)/shard_map/ppermute | solution.py:27
  69.0 4.4 %shard_map.85 = f32[1024,512]{1,0:T(8,128)S(1)} custom-call(f32[1024,512]{1,0:T(8,128)S(1)} %get-tuple-element.14.schur, f32[512,512]{1,0:T(8,128)S(1)} %collective-permute-done.1.got, s32[512,1]{1,0:T(8,128)S(1)} %copy.15.col_ref, s32[1,512]{1,0:T(1,128)S(1)} %get-tuple-element.17.row_ref, s32[1,1024]{1,0:T(1,128)S(1)} %bitcast.25), custom_call_target="tpu_custom_call" | custom-call | flops 2147483648 | bytes 5242880 | tf_op jit(solution)/shard_map/pallas_call | solution.py:165
  73.5 6.2 %all-to-all-done.1 = f32[8,128,512]{2,1,0:T(8,128)} async-done(((f32[8,128,512]{2,1,0:T(8,128)}), f32[8,128,512]{2,1,0:T(8,128)}, u32[]{:S(2)}, u32[]{:S(2)}) %all-to-all-start.1) | async-done | bytes 2097184 | tf_op jit(solution)/shard_map/all_to_all | solution.py:179
  79.6 51.5 %all_to_all.24 = f32[8,128,512]{2,1,0:T(8,128)S(1)} all-to-all(f32[8,128,512]{2,1,0:T(8,128)S(1)} %bitcast.21), channel_id=1, replica_groups=mesh['sx'=4,'sy'=8] {'sy'}, dimensions={0} | all-to-all | bytes 4194304 | tf_op jit(solution)/shard_map/all_to_all | solution.py:179
  131.1 4.1 %maximum_bitcast_fusion = f32[1,1,1024,1024]{3,2,1,0:T(8,128)} fusion(f32[1024,512]{1,0:T(8,128)} %bitcast.14, f32[1024,512]{1,0:T(8,128)S(1)} %bitcast.26), kind=kLoop, calls=%fused_computation | loop fusion | flops 1048576 | bytes 8388608 | tf_op jit(solution)/shard_map/broadcast_in_dim | solution.py:212
  (1 shorter events, 0.0 us)
Async XLA Ops:
  1.7 1.0 copy-start
  2.7 15.5 %copy-start.2 = (s32[1,1,1024]{2,1,0:T(1,128)S(1)}, s32[1,1,1024]{2,1,0:T(1,128)}, u32[]{:S(2)}) copy-start(s32[1,1,1024]{2,1,0:T(1,128)} %param.15) | copy-start | bytes 12292
  15.4 2.8 %collective-permute-start = (f32[512,512]{1,0:T(8,128)S(1)}, f32[512,512]{1,0:T(8,128)S(1)}, u32[]{:S(2)}, u32[]{:S(2)}) collective-permute-start(f32[512,512]{1,0:T(8,128)S(1)} %get-tuple-element.12), channel_id=1, source_target_pairs={{0,1},{1,0},{2,3},{3,2},{4,5},{5,4},{6,7},{7,6},{8,9},{9,8},{10,11... | collective-permute-start | bytes 3145736 | tf_op jit(solution)/shard_map/ppermute | solution.py:27
  24.0 6.6 %copy-start.3 = (s32[1,1,16,4]{2,3,1,0:T(4,128)S(1)}, s32[1,1,16,4]{2,3,1,0:T(4,128)}, u32[]{:S(2)}) copy-start(s32[1,1,16,4]{2,3,1,0:T(4,128)} %param.13) | copy-start | bytes 772
  24.0 6.7 %copy-start.1 = (bf16[1,1,16,128,128]{4,3,2,1,0:T(8,128)(2,1)S(1)}, bf16[1,1,16,128,128]{4,3,2,1,0:T(8,128)(2,1)}, u32[]{:S(2)}) copy-start(bf16[1,1,16,128,128]{4,3,2,1,0:T(8,128)(2,1)} %param.12) | copy-start | bytes 1572868
  24.0 55.6 %all-to-all-start.1 = ((f32[8,128,512]{2,1,0:T(8,128)}), f32[8,128,512]{2,1,0:T(8,128)}, u32[]{:S(2)}, u32[]{:S(2)}) async-start(f32[8,128,512]{2,1,0:T(8,128)} %bitcast.13), calls=%async_computation.1 | async-start | bytes 4194304 | tf_op jit(solution)/shard_map/all_to_all | solution.py:179
  43.4 25.6 %collective-permute-start.1 = (f32[512,512]{1,0:T(8,128)S(1)}, f32[512,512]{1,0:T(8,128)S(1)}, u32[]{:S(2)}, u32[]{:S(2)}) collective-permute-start(f32[512,512]{1,0:T(8,128)S(1)} %get-tuple-element.15), channel_id=1, source_target_pairs={{0,8},{8,0},{16,24},{24,16},{1,9},{9,1},{17,25},{25,17},{2,10},{10... | collective-permute-start | bytes 3145736 | tf_op jit(solution)/shard_map/ppermute | solution.py:27
